TPU v7x, 32 devices: a whole 2x2x4 slice. The times are simulated.
32 devices in a mesh: seq: 8 (over z, y), dp: 4 (over x, core).
Axes of the slice: x: 2, y: 2, z: 4, core: 2. Of those that a mesh axis runs over, the one named last changes fastest.
Arguments:
- query_heads: bfloat16 [4, 8, 256, 1536], P('dp', 'seq'), may hold values from -6 to 6
- key_heads: bfloat16 [4, 8, 256, 1536], P('dp', 'seq'), may hold values from -6 to 6
- value_heads: bfloat16 [4, 8, 256, 1536], P('dp', 'seq'), may hold values from -12 to 12
- cotangent: bfloat16 [4, 8, 256, 1536], P('dp', 'seq'), may hold values from -6 to 6
- out_gain: float32 [1536], replicated, may hold values from 2 to 8
- frame_counts: int32 [4, 4], P('dp'), may hold values from 1 to 4, 8 in all within a row
- live_patches: int32 [4, 4], P('dp'), may hold values from 64 to 256, as said below
Outputs:
- attended: bfloat16 [4, 8, 256, 1536], P('dp', 'seq')
- query_grad: bfloat16 [4, 8, 256, 1536], P('dp', 'seq')
- key_grad: bfloat16 [4, 8, 256, 1536], P('dp', 'seq')
- value_grad: bfloat16 [4, 8, 256, 1536], P('dp', 'seq')
- gain_grad: float32 [1536], replicated
Inputs may be any that keep to these rules, and one draw needn't show every extreme that they name: `live_patches`: in every replica some clip uses all 256 positions.
All inputs are finite; a program needn't handle non-finite values.
Results may differ from a plain program's by a relative error of at most 0.025.
Values may be sent and summed in bfloat16 or wider, within the bound.
A program may use at most 64 MiB of HBM per device.

v0:
```python
import functools
import math

import jax
import jax.numpy as jnp
from jax import lax
from jax.experimental import pallas as pl
from jax.experimental.pallas import tpu as pltpu
from jax.sharding import PartitionSpec as P

HEAD_DIM = 128
GROUP_HEADS = 2
LAG_TIME = 2
LAG_BACK = 2
SCALE = HEAD_DIM ** (-0.5)
EXP_SCALE = SCALE * math.log2(math.e)
EXCLUDED = -1e30
MESH = pl.DeviceIdType.MESH


def matmul(a, b, a_dim, b_dim):
    return lax.dot_general(
        a, b, (((a_dim,), (b_dim,)), ((), ())), preferred_element_type=jnp.float32
    )


def softmax(scores):
    weights = jnp.exp2((scores - jnp.max(scores, axis=-1, keepdims=True)) * EXP_SCALE)
    return weights * (1.0 / jnp.sum(weights, axis=-1, keepdims=True))


def score_grad(probs, prob_grad):
    inner = jnp.sum(probs * prob_grad, axis=-1, keepdims=True)
    return (probs * (prob_grad - inner)).astype(jnp.bfloat16)


def kernel(
    devices,
    replicas,
    counts_ref,
    live_ref,
    query_ref,
    key_ref,
    value_ref,
    grad_ref,
    gain_ref,
    attended_ref,
    query_grad_ref,
    key_grad_ref,
    value_grad_ref,
    gain_grad_ref,
    spatial,
    probs,
    moved,
    results,
    back,
    time_bias,
    time_live,
    space_live,
    gain_part,
    gain_dp,
    gain_seq,
    send_in,
    recv_in,
    send_out,
    recv_out,
    send_dp,
    recv_dp,
    send_seq,
    recv_seq,
):
    _, rows, channels = query_ref.shape
    patches = devices * rows
    width = GROUP_HEADS * HEAD_DIM
    groups = channels // width
    me = lax.axis_index("seq")
    my_replica = lax.axis_index("dp")

    def seq_peer(step):
        return lax.rem(me + step, devices)

    def dp_peer(step):
        return lax.rem(my_replica + step, replicas)

    barrier = pltpu.get_barrier_semaphore()

    @pl.loop(1, devices)
    def _(step):
        pl.semaphore_signal(
            barrier, inc=1, device_id={"seq": seq_peer(step)}, device_id_type=MESH
        )

    @pl.loop(1, replicas)
    def _(step):
        pl.semaphore_signal(
            barrier, inc=1, device_id={"dp": dp_peer(step)}, device_id_type=MESH
        )

    clips = counts_ref.shape[1]
    ends = []
    total = 0
    for c in range(clips):
        total = total + counts_ref[0, c]
        ends.append(total)

    def clip_of(frame):
        result = jnp.zeros_like(frame)
        for end in ends:
            result = result + jnp.where(frame >= end, 1, 0)
        return result

    def live_of(clip):
        result = jnp.zeros_like(clip)
        for c in range(clips):
            result = result + jnp.where(clip == c, live_ref[0, c], 0)
        return result

    row = lax.broadcasted_iota(jnp.int32, (patches, 1), 0)
    column = lax.broadcasted_iota(jnp.int32, (1, patches), 1)
    row_clip = clip_of(row // rows)
    column_clip = clip_of(column // rows)
    together = jnp.logical_and(row_clip == column_clip, row % rows == column % rows)
    time_bias[...] = jnp.where(together, 0.0, EXCLUDED)
    live_row = (me * rows + row % rows) < live_of(row_clip)
    time_live[...] = jnp.broadcast_to(jnp.where(live_row, 1.0, 0.0), time_live.shape)
    my_live_row = live_of(clip_of(jnp.full((patches, 1), me, jnp.int32)))
    my_live_column = live_of(clip_of(jnp.full((1, patches), me, jnp.int32)))
    space_live[...] = jnp.broadcast_to(jnp.where(row < my_live_row, 1.0, 0.0), space_live.shape)
    space_bias = jnp.where(column < my_live_column, 0.0, EXCLUDED)

    pl.semaphore_wait(barrier, devices + replicas - 2)

    def columns_of(group):
        return pl.ds(pl.multiple_of(group * width, width), width)

    def head_columns(group, h):
        return pl.ds(pl.multiple_of(group * width + h * HEAD_DIM, HEAD_DIM), HEAD_DIM)

    def send(source, target, array, group, send_sem, recv_sem):
        columns = columns_of(group)

        @pl.loop(1, devices)
        def _(step):
            peer = seq_peer(step)
            pltpu.make_async_remote_copy(
                src_ref=source.at[peer, :, columns],
                dst_ref=target.at[array, me, :, columns],
                send_sem=send_sem.at[group],
                recv_sem=recv_sem.at[group],
                device_id={"seq": peer},
                device_id_type=MESH,
            ).start()

    def wait_blocks(buffer, sem, group):
        part = buffer.at[:, pl.ds(0, devices - 1), :, columns_of(group)]
        pltpu.make_async_copy(part, part, sem.at[group]).wait()

    def flat(ref, columns):
        return ref[:, :, columns].reshape(patches, HEAD_DIM)

    def block(x):
        return x.astype(jnp.bfloat16).reshape(devices, rows, HEAD_DIM)

    def forward(group):
        columns = columns_of(group)
        for array, source in enumerate((query_ref, key_ref, grad_ref)):
            send(source, moved, array, group, send_in, recv_in)
            moved[array, me, :, columns] = source[me, :, columns]
        for h in range(GROUP_HEADS):
            head = head_columns(group, h)
            scores = matmul(flat(query_ref, head), flat(key_ref, head), 1, 1) + space_bias
            rounded = softmax(scores).astype(jnp.bfloat16)
            probs[group * GROUP_HEADS + h] = rounded
            result = matmul(rounded, flat(value_ref, head), 1, 0) * space_live[...]
            spatial[:, :, head] = block(result)
        send(spatial, moved, 3, group, send_in, recv_in)
        moved[3, me, :, columns] = spatial[me, :, columns]

    def temporal(group):
        wait_blocks(moved, recv_in, group)
        for h in range(GROUP_HEADS):
            head = head_columns(group, h)
            query = flat(moved.at[0], head)
            key = flat(moved.at[1], head)
            grad = flat(moved.at[2], head).astype(jnp.float32)
            value = flat(moved.at[3], head)
            gain = gain_ref[:, head]
            live = time_live[...]
            time_probs = softmax(matmul(query, key, 1, 1) + time_bias[...])
            rounded = time_probs.astype(jnp.bfloat16)
            result = matmul(rounded, value, 1, 0) * live
            results[0, :, :, head] = block(result * gain)
            gain_part[:, head] = jnp.sum(grad * result, axis=0, keepdims=True)
            grad_time = (grad * gain * live).astype(jnp.bfloat16)
            results[3, :, :, head] = block(matmul(rounded, grad_time, 0, 0))
            rounded_score = score_grad(time_probs, matmul(grad_time, value, 1, 1))
            results[1, :, :, head] = block(matmul(rounded_score, key, 1, 0) * SCALE)
            results[2, :, :, head] = block(matmul(rounded_score, query, 0, 0) * SCALE)
        columns = columns_of(group)
        for array in (3, 1, 2, 0):
            send(results.at[array], back, array, group, send_out, recv_out)
            back[array, me, :, columns] = results[array, me, :, columns]

    def backward(group):
        wait_blocks(back, recv_out, group)
        for h in range(GROUP_HEADS):
            head = head_columns(group, h)
            attended_ref[:, :, head] = back[0, :, :, head]
            grad = (flat(back.at[3], head).astype(jnp.float32) * space_live[...]).astype(jnp.bfloat16)
            rounded = probs[group * GROUP_HEADS + h]
            value_grad_ref[:, :, head] = block(matmul(rounded, grad, 0, 0))
            rounded_score = score_grad(
                rounded.astype(jnp.float32), matmul(grad, flat(value_ref, head), 1, 1)
            )
            query_grad_ref[:, :, head] = block(
                matmul(rounded_score, flat(key_ref, head), 1, 0) * SCALE
                + flat(back.at[1], head).astype(jnp.float32)
            )
            key_grad_ref[:, :, head] = block(
                matmul(rounded_score, flat(query_ref, head), 0, 0) * SCALE
                + flat(back.at[2], head).astype(jnp.float32)
            )

    def gain_over(axis, size, peer_of, mine, buffer, send_sem, recv_sem):
        buffer[mine] = gain_part[...]

        @pl.loop(1, size)
        def _(step):
            pltpu.make_async_remote_copy(
                src_ref=buffer.at[mine],
                dst_ref=buffer.at[mine],
                send_sem=send_sem,
                recv_sem=recv_sem,
                device_id={axis: peer_of(step)},
                device_id_type=MESH,
            ).start()

    def gain_sum(size, buffer, send_sem, recv_sem):
        part = buffer.at[pl.ds(0, size - 1)]
        pltpu.make_async_copy(part, part, recv_sem).wait()
        pltpu.make_async_copy(part, part, send_sem).wait()
        return jnp.sum(buffer[...], axis=0)

    last_time = groups - 1 + LAG_TIME

    @pl.loop(0, groups + LAG_TIME + LAG_BACK)
    def _(step):
        @pl.when(step < groups)
        def _():
            forward(step)

        @pl.when(jnp.logical_and(step >= LAG_TIME, step <= last_time))
        def _():
            temporal(step - LAG_TIME)

        @pl.when(step == last_time)
        def _():
            gain_over("dp", replicas, dp_peer, my_replica, gain_dp, send_dp, recv_dp)

        @pl.when(step == last_time + 1)
        def _():
            gain_part[...] = gain_sum(replicas, gain_dp, send_dp, recv_dp)
            gain_over("seq", devices, seq_peer, me, gain_seq, send_seq, recv_seq)

        @pl.when(step >= LAG_TIME + LAG_BACK)
        def _():
            backward(step - LAG_TIME - LAG_BACK)

    gain_grad_ref[...] = gain_sum(devices, gain_seq, send_seq, recv_seq)

    @pl.loop(0, groups)
    def _(group):
        wait_blocks(moved, send_in, group)
        wait_blocks(results, send_out, group)


def local(query_heads, key_heads, value_heads, cotangent, out_gain, frame_counts, live_patches):
    devices = lax.axis_size("seq")
    replicas = lax.axis_size("dp")
    _, local_frames, patches, channels = query_heads.shape
    assert local_frames == 1
    rows = patches // devices
    heads = channels // HEAD_DIM
    groups = heads // GROUP_HEADS
    blocks = (devices, rows, channels)
    vmem = pl.BlockSpec(memory_space=pltpu.VMEM)
    smem = pl.BlockSpec(memory_space=pltpu.SMEM)
    grid_out = jax.ShapeDtypeStruct(blocks, jnp.bfloat16)
    dma = pltpu.SemaphoreType.DMA
    outs = pl.pallas_call(
        functools.partial(kernel, devices, replicas),
        out_shape=[grid_out] * 4 + [jax.ShapeDtypeStruct((1, channels), jnp.float32)],
        in_specs=[smem, smem] + [vmem] * 5,
        out_specs=[vmem] * 5,
        scratch_shapes=[
            pltpu.VMEM(blocks, jnp.bfloat16),
            pltpu.VMEM((heads, patches, patches), jnp.bfloat16),
            pltpu.VMEM((4,) + blocks, jnp.bfloat16),
            pltpu.VMEM((4,) + blocks, jnp.bfloat16),
            pltpu.VMEM((4,) + blocks, jnp.bfloat16),
            pltpu.VMEM((patches, patches), jnp.float32),
            pltpu.VMEM((patches, HEAD_DIM), jnp.float32),
            pltpu.VMEM((patches, HEAD_DIM), jnp.float32),
            pltpu.VMEM((1, channels), jnp.float32),
            pltpu.VMEM((replicas, 1, channels), jnp.float32),
            pltpu.VMEM((devices, 1, channels), jnp.float32),
            dma((groups,)),
            dma((groups,)),
            dma((groups,)),
            dma((groups,)),
            dma,
            dma,
            dma,
            dma,
        ],
        compiler_params=pltpu.CompilerParams(
            collective_id=0, has_side_effects=True, vmem_limit_bytes=50 * 1024 * 1024
        ),
        cost_estimate=pl.CostEstimate(
            flops=28 * patches * patches * channels,
            bytes_accessed=16 * patches * channels,
            transcendentals=2 * heads * patches * patches,
        ),
    )(
        frame_counts,
        live_patches,
        query_heads.reshape(blocks),
        key_heads.reshape(blocks),
        value_heads.reshape(blocks),
        cotangent.reshape(blocks),
        out_gain.reshape(1, channels),
    )
    return tuple(x.reshape(query_heads.shape) for x in outs[:4]) + (outs[4].reshape(channels),)


def solution(mesh):
    split = P("dp", "seq", None, None)
    return jax.shard_map(
        local,
        mesh=mesh,
        in_specs=(split, split, split, split, P(), P("dp", None), P("dp", None)),
        out_specs=(split, split, split, split, P()),
        check_vma=False,
    )
```

profile of v0, /device:TPU:0, one launch (start us, length us, event | category | flops | bytes accessed | tf_op | source)
XLA Modules:
  0.0 152.6 jit_solution(5498426186737172824)
XLA Ops:
  0.6 0.7 reshape.44.gain_ref
  1.3 0.0 copy-start.1
  1.3 0.0 copy-start.2
  1.3 0.6 copy-done.1
  2.0 0.0 copy-done.2
  2.0 0.0 copy-start
  2.0 1.1 copy-done
  3.1 145.3 %shard_map.110 = (bf16[8,32,1536]{2,1,0:T(8,128)(2,1)S(1)}, bf16[8,32,1536]{2,1,0:T(8,128)(2,1)S(1)}, bf16[8,32,1536]{2,1,0:T(8,128)(2,1)S(1)}, bf16[8,32,1536]{2,1,0:T(8,128)(2,1)S(1)}, f32[1,1536]{1,0:T(1,128)S(1)}) custom-call(s32[1,4]{1,0:T(1,128)S(1)} %copy-done.1, s32[1,4]{1,0:T(1,128)S(1)} %copy-done.2, bf16[8,32,1536]{2,1,0:T(8,128)(2,1)S(1)} %bitcast.12, ...), custom_call_target="tpu_custom_call" | custom-call | flops 2818572288 | bytes 6291456 | tf_op jit(solution)/shard_map/pallas_call | solution.py:290
  148.4 0.6 reduce
  149.0 0.9 copy.16
  149.9 0.9 copy.17
  150.8 0.9 copy.18
  151.7 0.9 copy.19
Async XLA Ops:
  1.3 0.7 copy-start.1
  1.3 0.7 copy-start.2
  2.0 1.1 copy-start
where the time goes:
time: 153 us
  Pallas kernels  145 us (95%)
  local copies, waits for them, and re-layouts  6.02 us (4%)
    pallas_call x1, Pallas kernels, local(): pl.pallas_call(functools.partial(kernel, devices, replicas), out_shape=[g...  145 us
    unnamed x10, local copies, waits for them, and re-layouts  5.32 us

commit v1 on v0

--- a/solution.py
+++ b/solution.py
@@ -54,6 +54,7 @@
     moved,
     results,
     back,
+    back_across,
     time_bias,
     time_live,
     space_live,
@@ -64,17 +65,37 @@
     recv_in,
     send_out,
     recv_out,
+    send_in_across,
+    recv_in_across,
+    send_out_across,
+    recv_out_across,
     send_dp,
     recv_dp,
     send_seq,
     recv_seq,
 ):
-    _, rows, channels = query_ref.shape
+    half = devices // 2
+    quarter = half // 2
+    _, chunk_rows, channels = query_ref.shape
+    rows = chunk_rows // 2
     patches = devices * rows
     width = GROUP_HEADS * HEAD_DIM
     groups = channels // width
     me = lax.axis_index("seq")
     my_replica = lax.axis_index("dp")
+
+    side = me // half
+    place = me % half
+    left = side == 0
+    chunk = (place + quarter) % half
+    inner = jnp.logical_or(
+        jnp.logical_and(left, place >= quarter),
+        jnp.logical_and(jnp.logical_not(left), place < quarter),
+    )
+    edge = jnp.logical_or(me == 0, me == devices - 1)
+
+    def side_peer(step):
+        return side * half + lax.rem(place + step, half)
 
     def seq_peer(step):
         return lax.rem(me + step, devices)
@@ -121,13 +142,41 @@
     column_clip = clip_of(column // rows)
     together = jnp.logical_and(row_clip == column_clip, row % rows == column % rows)
     time_bias[...] = jnp.where(together, 0.0, EXCLUDED)
-    live_row = (me * rows + row % rows) < live_of(row_clip)
-    time_live[...] = jnp.broadcast_to(jnp.where(live_row, 1.0, 0.0), time_live.shape)
+    row_first = jnp.zeros_like(row)
+    row_last = jnp.zeros_like(row)
+    first = 0
+    for c in range(clips):
+        row_first = row_first + jnp.where(row_clip == c, first, 0)
+        row_last = row_last + jnp.where(row_clip == c, ends[c] - 1, 0)
+        first = ends[c]
+    first_left = jnp.where(row_first < half, 1, 0)
+    last_left = jnp.where(row_last < half, 1, 0)
+    is_inner = jnp.where(inner, 1, 0)
+    left_mine = is_inner * first_left + (1 - is_inner) * last_left
+    right_mine = is_inner * (1 - last_left) + (1 - is_inner) * (1 - first_left)
+    mine = (1 - side) * left_mine + side * right_mine
+    for part in range(2):
+        position = chunk * chunk_rows + part * rows + row % rows
+        keep = mine * jnp.where(position < live_of(row_clip), 1, 0)
+        time_live[part] = jnp.broadcast_to(keep.astype(jnp.float32), time_live.shape[1:])
     my_live_row = live_of(clip_of(jnp.full((patches, 1), me, jnp.int32)))
     my_live_column = live_of(clip_of(jnp.full((1, patches), me, jnp.int32)))
     space_live[...] = jnp.broadcast_to(jnp.where(row < my_live_row, 1.0, 0.0), space_live.shape)
     space_bias = jnp.where(column < my_live_column, 0.0, EXCLUDED)
 
+    far = (1 - side) * (devices - 1)
+    unused = jnp.where(inner, far, (1 - side) * half)
+    unused_end = jnp.where(inner, far + 1, (1 - side) * half + half)
+
+    @pl.loop(unused, unused_end)
+    def _(frame):
+        for array in range(4):
+            moved[array, frame] = jnp.zeros(moved.shape[2:], moved.dtype)
+
+    @pl.when(edge)
+    def _():
+        back_across[...] = jnp.zeros_like(back_across)
+
     pl.semaphore_wait(barrier, devices + replicas - 2)
 
     def columns_of(group):
@@ -136,36 +185,71 @@
     def head_columns(group, h):
         return pl.ds(pl.multiple_of(group * width + h * HEAD_DIM, HEAD_DIM), HEAD_DIM)
 
-    def send(source, target, array, group, send_sem, recv_sem):
+    def start(source, target, send_sem, recv_sem, peer):
+        pltpu.make_async_remote_copy(
+            src_ref=source,
+            dst_ref=target,
+            send_sem=send_sem,
+            recv_sem=recv_sem,
+            device_id={"seq": peer},
+            device_id_type=MESH,
+        ).start()
+
+    def send_inputs(source, array, group):
         columns = columns_of(group)
-
-        @pl.loop(1, devices)
+        target = moved.at[array, me, :, columns]
+
+        @pl.when(jnp.logical_not(edge))
+        def _():
+            @pl.loop(0, quarter)
+            def _(step):
+                peer = jnp.where(left, half, quarter) + lax.rem(place + step, quarter)
+                held = source.at[(peer % half + quarter) % half, :, columns]
+                start(held, target, send_in_across.at[group], recv_in_across.at[group], peer)
+
+        @pl.loop(1, half)
         def _(step):
-            peer = seq_peer(step)
-            pltpu.make_async_remote_copy(
-                src_ref=source.at[peer, :, columns],
-                dst_ref=target.at[array, me, :, columns],
-                send_sem=send_sem.at[group],
-                recv_sem=recv_sem.at[group],
-                device_id={"seq": peer},
-                device_id_type=MESH,
-            ).start()
-
-    def wait_blocks(buffer, sem, group):
-        part = buffer.at[:, pl.ds(0, devices - 1), :, columns_of(group)]
+            peer = side_peer(step)
+            held = source.at[(peer % half + quarter) % half, :, columns]
+            start(held, target, send_in.at[group], recv_in.at[group], peer)
+
+        moved[array, me, :, columns] = source[chunk, :, columns]
+
+    def send_results(array, group):
+        columns = columns_of(group)
+
+        @pl.when(inner)
+        def _():
+            target = back_across.at[array, chunk % quarter, :, columns]
+
+            @pl.loop(0, half - 1)
+            def _(step):
+                peer = jnp.where(left, half, 1) + lax.rem(place + step, half - 1)
+                held = results.at[array, peer, :, columns]
+                start(held, target, send_out_across.at[group], recv_out_across.at[group], peer)
+
+        @pl.loop(1, half)
+        def _(step):
+            peer = side_peer(step)
+            held = results.at[array, peer, :, columns]
+            target = back.at[array, chunk, :, columns]
+            start(held, target, send_out.at[group], recv_out.at[group], peer)
+
+        back[array, chunk, :, columns] = results[array, me, :, columns]
+
+    def wait_blocks(count, sem, group):
+        part = moved.at[:, pl.ds(0, count), :, columns_of(group)]
         pltpu.make_async_copy(part, part, sem.at[group]).wait()
 
     def flat(ref, columns):
         return ref[:, :, columns].reshape(patches, HEAD_DIM)
 
     def block(x):
-        return x.astype(jnp.bfloat16).reshape(devices, rows, HEAD_DIM)
+        return x.astype(jnp.bfloat16).reshape(half, chunk_rows, HEAD_DIM)
 
     def forward(group):
-        columns = columns_of(group)
         for array, source in enumerate((query_ref, key_ref, grad_ref)):
-            send(source, moved, array, group, send_in, recv_in)
-            moved[array, me, :, columns] = source[me, :, columns]
+            send_inputs(source, array, group)
         for h in range(GROUP_HEADS):
             head = head_columns(group, h)
             scores = matmul(flat(query_ref, head), flat(key_ref, head), 1, 1) + space_bias
@@ -173,36 +257,61 @@
             probs[group * GROUP_HEADS + h] = rounded
             result = matmul(rounded, flat(value_ref, head), 1, 0) * space_live[...]
             spatial[:, :, head] = block(result)
-        send(spatial, moved, 3, group, send_in, recv_in)
-        moved[3, me, :, columns] = spatial[me, :, columns]
+        send_inputs(spatial, 3, group)
 
     def temporal(group):
-        wait_blocks(moved, recv_in, group)
+        wait_blocks(half - 1, recv_in, group)
+
+        @pl.when(inner)
+        def _():
+            wait_blocks(half - 1, recv_in_across, group)
+
         for h in range(GROUP_HEADS):
             head = head_columns(group, h)
-            query = flat(moved.at[0], head)
-            key = flat(moved.at[1], head)
-            grad = flat(moved.at[2], head).astype(jnp.float32)
-            value = flat(moved.at[3], head)
             gain = gain_ref[:, head]
-            live = time_live[...]
-            time_probs = softmax(matmul(query, key, 1, 1) + time_bias[...])
-            rounded = time_probs.astype(jnp.bfloat16)
-            result = matmul(rounded, value, 1, 0) * live
-            results[0, :, :, head] = block(result * gain)
-            gain_part[:, head] = jnp.sum(grad * result, axis=0, keepdims=True)
-            grad_time = (grad * gain * live).astype(jnp.bfloat16)
-            results[3, :, :, head] = block(matmul(rounded, grad_time, 0, 0))
-            rounded_score = score_grad(time_probs, matmul(grad_time, value, 1, 1))
-            results[1, :, :, head] = block(matmul(rounded_score, key, 1, 0) * SCALE)
-            results[2, :, :, head] = block(matmul(rounded_score, query, 0, 0) * SCALE)
+            total_gain = jnp.zeros((1, HEAD_DIM), jnp.float32)
+            for part in range(2):
+                inside = pl.ds(part * rows, rows)
+
+                def load(array):
+                    return moved[array, :, inside, head].reshape(patches, HEAD_DIM)
+
+                def store(array, x):
+                    x = x.astype(jnp.bfloat16).reshape(devices, rows, HEAD_DIM)
+                    results[array, :, inside, head] = x
+
+                query = load(0)
+                key = load(1)
+                grad = load(2).astype(jnp.float32)
+                value = load(3)
+                live = time_live[part]
+                time_probs = softmax(matmul(query, key, 1, 1) + time_bias[...])
+                rounded = time_probs.astype(jnp.bfloat16)
+                result = matmul(rounded, value, 1, 0) * live
+                store(0, result * gain)
+                total_gain = total_gain + jnp.sum(grad * result, axis=0, keepdims=True)
+                grad_time = (grad * gain * live).astype(jnp.bfloat16)
+                store(3, matmul(rounded, grad_time, 0, 0))
+                rounded_score = score_grad(time_probs, matmul(grad_time, value, 1, 1))
+                store(1, matmul(rounded_score, key, 1, 0) * SCALE)
+                store(2, matmul(rounded_score, query, 0, 0) * SCALE)
+            gain_part[:, head] = total_gain
+        for array in (3, 1, 2, 0):
+            send_results(array, group)
+
+    def backward(group):
+        wait_blocks(half - 1, recv_out, group)
+
+        @pl.when(jnp.logical_not(edge))
+        def _():
+            wait_blocks(quarter, recv_out_across, group)
+
         columns = columns_of(group)
-        for array in (3, 1, 2, 0):
-            send(results.at[array], back, array, group, send_out, recv_out)
-            back[array, me, :, columns] = results[array, me, :, columns]
-
-    def backward(group):
-        wait_blocks(back, recv_out, group)
+        across = pl.ds(jnp.where(left, quarter, 0), quarter)
+        for array in range(4):
+            near = back[array, across, :, columns].astype(jnp.float32)
+            other = back_across[array, :, :, columns].astype(jnp.float32)
+            back[array, across, :, columns] = (near + other).astype(jnp.bfloat16)
         for h in range(GROUP_HEADS):
             head = head_columns(group, h)
             attended_ref[:, :, head] = back[0, :, :, head]
@@ -270,8 +379,16 @@
 
     @pl.loop(0, groups)
     def _(group):
-        wait_blocks(moved, send_in, group)
-        wait_blocks(results, send_out, group)
+        wait_blocks(half - 1, send_in, group)
+        wait_blocks(half - 1, send_out, group)
+
+        @pl.when(jnp.logical_not(edge))
+        def _():
+            wait_blocks(quarter, send_in_across, group)
+
+        @pl.when(inner)
+        def _():
+            wait_blocks(half - 1, send_out_across, group)
 
 
 def local(query_heads, key_heads, value_heads, cotangent, out_gain, frame_counts, live_patches):
@@ -279,10 +396,12 @@
     replicas = lax.axis_size("dp")
     _, local_frames, patches, channels = query_heads.shape
     assert local_frames == 1
-    rows = patches // devices
+    chunks = devices // 2
+    rows = patches // chunks
     heads = channels // HEAD_DIM
     groups = heads // GROUP_HEADS
-    blocks = (devices, rows, channels)
+    blocks = (chunks, rows, channels)
+    frames = (4, devices, rows, channels)
     vmem = pl.BlockSpec(memory_space=pltpu.VMEM)
     smem = pl.BlockSpec(memory_space=pltpu.SMEM)
     grid_out = jax.ShapeDtypeStruct(blocks, jnp.bfloat16)
@@ -295,15 +414,20 @@
         scratch_shapes=[
             pltpu.VMEM(blocks, jnp.bfloat16),
             pltpu.VMEM((heads, patches, patches), jnp.bfloat16),
+            pltpu.VMEM(frames, jnp.bfloat16),
+            pltpu.VMEM(frames, jnp.bfloat16),
             pltpu.VMEM((4,) + blocks, jnp.bfloat16),
-            pltpu.VMEM((4,) + blocks, jnp.bfloat16),
-            pltpu.VMEM((4,) + blocks, jnp.bfloat16),
+            pltpu.VMEM((4, chunks // 2, rows, channels), jnp.bfloat16),
             pltpu.VMEM((patches, patches), jnp.float32),
-            pltpu.VMEM((patches, HEAD_DIM), jnp.float32),
+            pltpu.VMEM((2, patches, HEAD_DIM), jnp.float32),
             pltpu.VMEM((patches, HEAD_DIM), jnp.float32),
             pltpu.VMEM((1, channels), jnp.float32),
             pltpu.VMEM((replicas, 1, channels), jnp.float32),
             pltpu.VMEM((devices, 1, channels), jnp.float32),
+            dma((groups,)),
+            dma((groups,)),
+            dma((groups,)),
+            dma((groups,)),
             dma((groups,)),
             dma((groups,)),
             dma((groups,)),

time: 153 us -> 143 us (0.935)
  Pallas kernels: 145 us -> 135 us
    pallas_call x1, Pallas kernels: 145 us -> 135 us  [local(): pl.pallas_call(functools.partial(kernel, devices, replicas), out_shape=[g...]
where the time goes in v1:
time: 143 us
  Pallas kernels  135 us (94%)
  local copies, waits for them, and re-layouts  6.02 us (4%)
    pallas_call x1, Pallas kernels, local(): pl.pallas_call(functools.partial(kernel, devices, replicas), out_shape=[g...  135 us
    unnamed x10, local copies, waits for them, and re-layouts  5.32 us

profile of v1, /device:TPU:0, one launch (start us, length us, event | category | flops | bytes accessed | tf_op | source)
XLA Modules:
  0.0 142.7 jit_solution(12475245749958080826)
XLA Ops:
  0.6 0.7 reshape.44.gain_ref
  1.3 0.0 copy-start.1
  1.3 0.0 copy-start.2
  1.3 0.6 copy-done.1
  2.0 0.0 copy-done.2
  2.0 0.0 copy-start
  2.0 1.1 copy-done
  3.1 135.4 %shard_map.110 = (bf16[4,64,1536]{2,1,0:T(8,128)(2,1)S(1)}, bf16[4,64,1536]{2,1,0:T(8,128)(2,1)S(1)}, bf16[4,64,1536]{2,1,0:T(8,128)(2,1)S(1)}, bf16[4,64,1536]{2,1,0:T(8,128)(2,1)S(1)}, f32[1,1536]{1,0:T(1,128)S(1)}) custom-call(s32[1,4]{1,0:T(1,128)S(1)} %copy-done.1, s32[1,4]{1,0:T(1,128)S(1)} %copy-done.2, bf16[4,64,1536]{2,1,0:T(8,128)(2,1)S(1)} %bitcast.12, ...), custom_call_target="tpu_custom_call" | custom-call | flops 2818572288 | bytes 6291456 | tf_op jit(solution)/shard_map/pallas_call | solution.py:409
  138.5 0.6 reduce
  139.1 0.9 copy.16
  140.0 0.9 copy.17
  140.9 0.9 copy.18
  141.8 0.9 copy.19
Async XLA Ops:
  1.3 0.7 copy-start.1
  1.3 0.7 copy-start.2
  2.0 1.1 copy-start

commit v2 on v1

--- a/solution.py
+++ b/solution.py
@@ -9,8 +9,8 @@
 from jax.sharding import PartitionSpec as P
 
 HEAD_DIM = 128
-GROUP_HEADS = 2
-LAG_TIME = 2
+GROUP_HEADS = 1
+LAG_TIME = 5
 LAG_BACK = 2
 SCALE = HEAD_DIM ** (-0.5)
 EXP_SCALE = SCALE * math.log2(math.e)

time: 143 us -> 139 us (0.972)
  Pallas kernels: 135 us -> 131 us
    pallas_call x1, Pallas kernels: 135 us -> 131 us  [local(): pl.pallas_call(functools.partial(kernel, devices, replicas), out_shape=[g...]
where the time goes in v2:
time: 139 us; the launch traced here: 138 us
  Pallas kernels  131 us (94%)
  local copies, waits for them, and re-layouts  6.02 us (4%)
    pallas_call x1, Pallas kernels, local(): pl.pallas_call(functools.partial(kernel, devices, replicas), out_shape=[g...  131 us
    unnamed x10, local copies, waits for them, and re-layouts  5.32 us

profile of v2, /device:TPU:0, one launch (start us, length us, event | category | flops | bytes accessed | tf_op | source)
XLA Modules:
  0.0 138.3 jit_solution(1104810161410166771)
XLA Ops:
  0.6 0.7 reshape.44.gain_ref
  1.3 0.0 copy-start.1
  1.3 0.0 copy-start.2
  1.3 0.6 copy-done.1
  2.0 0.0 copy-done.2
  2.0 0.0 copy-start
  2.0 1.1 copy-done
  3.1 131.0 %shard_map.110 = (bf16[4,64,1536]{2,1,0:T(8,128)(2,1)S(1)}, bf16[4,64,1536]{2,1,0:T(8,128)(2,1)S(1)}, bf16[4,64,1536]{2,1,0:T(8,128)(2,1)S(1)}, bf16[4,64,1536]{2,1,0:T(8,128)(2,1)S(1)}, f32[1,1536]{1,0:T(1,128)S(1)}) custom-call(s32[1,4]{1,0:T(1,128)S(1)} %copy-done.1, s32[1,4]{1,0:T(1,128)S(1)} %copy-done.2, bf16[4,64,1536]{2,1,0:T(8,128)(2,1)S(1)} %bitcast.12, ...), custom_call_target="tpu_custom_call" | custom-call | flops 2818572288 | bytes 6291456 | tf_op jit(solution)/shard_map/pallas_call | solution.py:409
  134.1 0.6 reduce
  134.8 0.9 copy.16
  135.6 0.9 copy.17
  136.5 0.9 copy.18
  137.4 0.9 copy.19
Async XLA Ops:
  1.3 0.7 copy-start.1
  1.3 0.7 copy-start.2
  2.0 1.1 copy-start

commit v3 on v2

--- a/solution.py
+++ b/solution.py
@@ -268,7 +268,7 @@
 
         for h in range(GROUP_HEADS):
             head = head_columns(group, h)
-            gain = gain_ref[:, head]
+            gain = gain_ref[head].reshape(1, HEAD_DIM)
             total_gain = jnp.zeros((1, HEAD_DIM), jnp.float32)
             for part in range(2):
                 inside = pl.ds(part * rows, rows)
@@ -375,7 +375,9 @@
         def _():
             backward(step - LAG_TIME - LAG_BACK)
 
-    gain_grad_ref[...] = gain_sum(devices, gain_seq, send_seq, recv_seq)
+    gain_total = gain_sum(devices, gain_seq, send_seq, recv_seq)
+    for first in range(0, channels, HEAD_DIM):
+        gain_grad_ref[pl.ds(first, HEAD_DIM)] = gain_total[0, first : first + HEAD_DIM]
 
     @pl.loop(0, groups)
     def _(group):
@@ -408,7 +410,7 @@
     dma = pltpu.SemaphoreType.DMA
     outs = pl.pallas_call(
         functools.partial(kernel, devices, replicas),
-        out_shape=[grid_out] * 4 + [jax.ShapeDtypeStruct((1, channels), jnp.float32)],
+        out_shape=[grid_out] * 4 + [jax.ShapeDtypeStruct((channels,), jnp.float32)],
         in_specs=[smem, smem] + [vmem] * 5,
         out_specs=[vmem] * 5,
         scratch_shapes=[
@@ -452,9 +454,9 @@
         key_heads.reshape(blocks),
         value_heads.reshape(blocks),
         cotangent.reshape(blocks),
-        out_gain.reshape(1, channels),
+        out_gain,
     )
-    return tuple(x.reshape(query_heads.shape) for x in outs[:4]) + (outs[4].reshape(channels),)
+    return tuple(x.reshape(query_heads.shape) for x in outs[:4]) + (outs[4],)
 
 
 def solution(mesh):

time: 139 us -> 138 us (level)
    unnamed x10 -> x13, local copies, waits for them, and re-layouts: 5.32 us -> 6.6 us
where the time goes in v3:
time: 138 us
  Pallas kernels  131 us (95%)
  local copies, waits for them, and re-layouts  6.6 us (5%)
    pallas_call x1, Pallas kernels, local(): pl.pallas_call(functools.partial(kernel, devices, replicas), out_shape=[g...  131 us
    unnamed x13, local copies, waits for them, and re-layouts  6.6 us

profile of v3, /device:TPU:0, one launch (start us, length us, event | category | flops | bytes accessed | tf_op | source)
XLA Modules:
  0.0 138.2 jit_solution(10225614418995361671)
XLA Ops:
  0.6 0.0 copy-start.2
  0.6 0.0 copy-start.3
  0.7 0.6 copy-done.2
  1.3 0.0 copy-done.3
  1.3 0.0 copy-start
  1.3 1.1 copy-done
  2.4 0.0 copy-start.1
  2.4 0.7 copy-done.1
  3.1 131.0 %shard_map.110 = (bf16[4,64,1536]{2,1,0:T(8,128)(2,1)S(1)}, bf16[4,64,1536]{2,1,0:T(8,128)(2,1)S(1)}, bf16[4,64,1536]{2,1,0:T(8,128)(2,1)S(1)}, bf16[4,64,1536]{2,1,0:T(8,128)(2,1)S(1)}, f32[1536]{0:T(1024)S(1)}) custom-call(s32[1,4]{1,0:T(1,128)S(1)} %copy-done.2, s32[1,4]{1,0:T(1,128)S(1)} %copy-done.3, bf16[4,64,1536]{2,1,0:T(8,128)(2,1)S(1)} %bitcast.12, ...), custom_call_target="tpu_custom_call" | custom-call | flops 2818572288 | bytes 6291456 | tf_op jit(solution)/shard_map/pallas_call | solution.py:411
  134.1 0.9 copy.17
  135.0 0.9 copy.18
  135.9 0.9 copy.19
  136.8 0.9 copy.20
  137.6 0.6 copy.21
Async XLA Ops:
  0.6 0.7 copy-start.2
  0.6 0.7 copy-start.3
  1.3 1.1 copy-start
  2.4 0.7 copy-start.1
